TPU v7x, 32 devices: a whole 2x2x4 slice. The times are simulated.
32 devices in a mesh: groups: 2 (over y), tok: 4 (over z), head: 2 (over x), sub: 2 (over core).
Axes of the slice: x: 2, y: 2, z: 4, core: 2. Of those that a mesh axis runs over, the one named last changes fastest.
Arguments:
- in_tokens: bfloat16 [16384, 768], P(('groups', 'tok', 'sub')), parts along dimension 0, may hold values from -6 to 6
- target_views: int32 [3072], P(('groups', 'tok', 'sub')), parts along dimension 0, may hold values from 0 to 31
- target_rays: int32 [3072], P(('groups', 'tok', 'sub')), parts along dimension 0, may hold values from 0 to 1023
- camera_turn: float32 [64, 9], P('groups'), parts along dimension 0, may hold values from -0.15 to 0.15
- camera_anchor: float32 [64, 3], P('groups'), parts along dimension 0, may hold values from -4 to 4
- pixels_true: bfloat16 [16, 2, 96, 192], P(('groups', 'tok', 'sub'), 'head'), parts along dimension 0, may hold values from 0 to 1
- transient: int32 [16, 2, 96, 64], P(('groups', 'tok', 'sub'), 'head'), parts along dimension 0, may hold values 0 or 1
- query_weight: bfloat16 [768, 384], P(None, 'head'), may hold values from -0.21875 to 0.21875
- key_weight: bfloat16 [768, 384], P(None, 'head'), may hold values from -0.21875 to 0.21875
- value_weight: bfloat16 [768, 384], P(None, 'head'), may hold values from -0.21875 to 0.21875
- rate_weight: bfloat16 [768, 2], P(None, 'head'), may hold values from -0.21875 to 0.21875
- rate_bias: float32 [2], P('head'), may hold values from -1 to 1
- fast_init: bfloat16 [2, 3, 192, 384], P('head'), may hold values from -0.4375 to 0.4375
- out_weight: bfloat16 [384, 768], P('head'), may hold values from -0.3125 to 0.3125
- ray_weight: bfloat16 [384, 768], replicated, may hold values from -0.3125 to 0.3125
- norm_gain: float32 [768], replicated, may hold values from 0.1 to 1.9
- wide_weight: bfloat16 [768, 1536], P(None, 'head'), may hold values from -0.21875 to 0.21875
- narrow_weight: bfloat16 [768, 1536], P(None, 'head'), may hold values from -0.15625 to 0.15625
- decode_gain: float32 [768], replicated, may hold values from 0.1 to 1.9
- decode_weight: bfloat16 [768, 256], replicated, may hold values from -0.21875 to 0.21875
Outputs:
- render: bfloat16 [16, 2, 96, 192], P(('groups', 'tok', 'sub'), 'head'), parts along dimension 0
- grad_decode: float32 [1536, 256], P(('groups', 'tok', 'sub')), parts along dimension 0
- grad_narrow: float32 [1536, 1536], P(('groups', 'tok', 'sub'), 'head'), parts along dimension 0
There are 2 independent parts, one for each index of `groups`. A program takes and returns all parts, laid end to end along the dimension named above; an argument that names none is the same for every part. Nothing has to cross between parts.
Inputs may be any that keep to these rules, and one draw needn't show every extreme that they name: `transient`: 1 marks a pixel to leave out of the loss. `target_views`: index of the target token's camera. `target_rays`: index of the target token's patch, row-major over the image's patches.
All inputs are finite; a program needn't handle non-finite values. No bound on the sum of `transient` on one device may be relied on, other than what follows from the above.
Results may differ from a plain program's by a relative error of at most 0.024.
Values may be sent and summed in bfloat16 or wider, within the bound.
A program may use at most 64 MiB of HBM per device.

v0:
```python
import math

import jax
import jax.numpy as jnp
from jax import lax
from jax.sharding import PartitionSpec as P

PATCH = 8
IMG = 256


EPSILON = 1e-06
RATE_SCALE = 0.2
BETA_FLOOR = 0.05


def rms_scale(vector):
    return lax.rsqrt(jnp.mean(vector * vector, axis=-1, keepdims=True) + EPSILON)


def silu_grad(activation_in):
    sigmoid_part = jax.nn.sigmoid(activation_in)
    return sigmoid_part * (1.0 + activation_in * (1.0 - sigmoid_part))


def plucker_rays(view_ids, ray_ids, camera_turn, camera_anchor):
    camera_count = camera_turn.shape[0]
    one_hot = view_ids[:, None] == jnp.arange(camera_count, dtype=jnp.int32)[None, :]
    turn_rows = jnp.sum(jnp.where(one_hot[:, :, None], camera_turn[None, :, :], 0.0), axis=1)
    anchor_rows = jnp.sum(jnp.where(one_hot[:, :, None], camera_anchor[None, :, :], 0.0), axis=1)
    patch_across = IMG // PATCH
    patch_row = ray_ids // patch_across
    patch_col = ray_ids % patch_across
    pixel_index = jnp.arange(PATCH * PATCH, dtype=jnp.int32)
    column_pos = (patch_col[:, None] * PATCH + pixel_index[None, :] % PATCH).astype(
        jnp.float32
    ) + 0.5
    row_pos = (patch_row[:, None] * PATCH + pixel_index[None, :] // PATCH).astype(jnp.float32) + 0.5
    camera_x = (column_pos - 0.5 * IMG) / IMG
    camera_y = (row_pos - 0.5 * IMG) / IMG
    dir_x = (1.0 + turn_rows[:, 0:1]) * camera_x + turn_rows[:, 1:2] * camera_y + turn_rows[:, 2:3]
    dir_y = turn_rows[:, 3:4] * camera_x + (1.0 + turn_rows[:, 4:5]) * camera_y + turn_rows[:, 5:6]
    dir_z = turn_rows[:, 6:7] * camera_x + turn_rows[:, 7:8] * camera_y + (1.0 + turn_rows[:, 8:9])
    norm_inv = lax.rsqrt(dir_x * dir_x + dir_y * dir_y + dir_z * dir_z)
    dir_x = dir_x * norm_inv
    dir_y = dir_y * norm_inv
    dir_z = dir_z * norm_inv
    anchor_x = anchor_rows[:, 0:1]
    anchor_y = anchor_rows[:, 1:2]
    anchor_z = anchor_rows[:, 2:3]
    moment_x = anchor_y * dir_z - anchor_z * dir_y
    moment_y = anchor_z * dir_x - anchor_x * dir_z
    moment_z = anchor_x * dir_y - anchor_y * dir_x
    return jnp.concatenate([dir_x, dir_y, dir_z, moment_x, moment_y, moment_z], axis=1).astype(
        jnp.bfloat16
    )


def fast_gradient(keys_normed, value_rows, rate_rows, weights):
    pre_first = jnp.dot(keys_normed, weights[0], preferred_element_type=jnp.float32)
    pre_third = jnp.dot(keys_normed, weights[1], preferred_element_type=jnp.float32)
    fast_hidden = (jax.nn.silu(pre_first) * pre_third).astype(jnp.bfloat16)
    descent = (-rate_rows[:, None] * value_rows.astype(jnp.float32)).astype(jnp.bfloat16)
    contract_rows = (((0,), (0,)), ((), ()))
    grad_second = lax.dot_general(
        descent, fast_hidden, contract_rows, preferred_element_type=jnp.float32
    )
    grad_hidden = jnp.dot(descent, weights[2], preferred_element_type=jnp.float32)
    grad_pre_first = (grad_hidden * pre_third * silu_grad(pre_first)).astype(jnp.bfloat16)
    grad_pre_third = (grad_hidden * jax.nn.silu(pre_first)).astype(jnp.bfloat16)
    grad_first = lax.dot_general(
        keys_normed, grad_pre_first, contract_rows, preferred_element_type=jnp.float32
    )
    grad_third = lax.dot_general(
        keys_normed, grad_pre_third, contract_rows, preferred_element_type=jnp.float32
    )
    return jnp.stack([grad_first, grad_third, grad_second])


def renormalize(gradient, start_rows):
    start_float = start_rows.astype(jnp.float32)
    moved_rows = start_float - gradient
    restore = jnp.sqrt(jnp.mean(start_float * start_float, axis=-1, keepdims=True) + EPSILON)
    return (moved_rows * rms_scale(moved_rows) * restore).astype(jnp.bfloat16)


def apply_fast(query_rows, weights):
    apply_first = jnp.dot(query_rows, weights[0], preferred_element_type=jnp.float32)
    apply_third = jnp.dot(query_rows, weights[1], preferred_element_type=jnp.float32)
    apply_hidden = (jax.nn.silu(apply_first) * apply_third).astype(jnp.bfloat16)
    contract_last = (((1,), (1,)), ((), ()))
    return lax.dot_general(
        apply_hidden, weights[2], contract_last, preferred_element_type=jnp.float32
    ).astype(jnp.bfloat16)


def pixel_loss(logits, truth_rows, transient_bits, loss_scale):
    pixel_count = transient_bits.shape[-1]
    row_total = logits.shape[0]
    colors = logits[:, : 3 * pixel_count]
    spread_logit = logits[:, 3 * pixel_count :]
    spread = jax.nn.softplus(spread_logit) + BETA_FLOOR
    error_rows = colors.reshape(row_total, pixel_count, 3) - truth_rows.reshape(
        row_total, pixel_count, 3
    ).astype(jnp.float32)
    squared = jnp.sum(error_rows * error_rows, axis=2)
    keep_mask = (1 - transient_bits).astype(jnp.float32)
    inverse = 1.0 / (spread * spread)
    grad_colors = (keep_mask * inverse * loss_scale)[:, :, None] * error_rows
    grad_spread = (
        keep_mask
        * (1.0 / spread - squared * inverse / spread)
        * loss_scale
        * jax.nn.sigmoid(spread_logit)
    )
    grad_logits = jnp.concatenate(
        [grad_colors.reshape(row_total, 3 * pixel_count), grad_spread], axis=1
    ).astype(jnp.bfloat16)
    return (colors.astype(jnp.bfloat16), grad_logits)


def on_device(
    in_tokens,
    target_views,
    target_rays,
    camera_turn,
    camera_anchor,
    pixels_true,
    transient,
    query_weight,
    key_weight,
    value_weight,
    rate_weight,
    rate_bias,
    fast_init,
    out_weight,
    ray_weight,
    norm_gain,
    wide_weight,
    narrow_weight,
    decode_gain,
    decode_weight,
):
    token_devices = lax.axis_size("tok") * lax.axis_size("sub")
    in_total = in_tokens.shape[0] * token_devices
    target_total = target_views.shape[0] * token_devices
    contract_last = (((1,), (1,)), ((), ()))
    contract_rows = (((0,), (0,)), ((), ()))
    keys_raw = jnp.dot(in_tokens, key_weight, preferred_element_type=jnp.float32)
    keys_normed = (keys_raw * rms_scale(keys_raw)).astype(jnp.bfloat16)
    value_rows = jnp.dot(in_tokens, value_weight, preferred_element_type=jnp.float32).astype(
        jnp.bfloat16
    )
    rate_logit = jnp.dot(in_tokens, rate_weight, preferred_element_type=jnp.float32) + rate_bias
    rate_rows = jax.nn.softplus(rate_logit[:, 0]) * (RATE_SCALE / math.sqrt(in_total))
    start_weights = fast_init[0]
    local_grads = fast_gradient(keys_normed, value_rows, rate_rows, start_weights)
    owned_share = lax.psum_scatter(local_grads, ("tok", "sub"), scatter_dimension=1, tiled=True)
    row_count = owned_share.shape[1]
    first_row = lax.axis_index(("tok", "sub")) * row_count
    fresh_rows = renormalize(
        owned_share, lax.dynamic_slice_in_dim(start_weights, first_row, row_count, 1)
    )
    new_weights = lax.all_gather(fresh_rows, ("tok", "sub"), axis=1, tiled=True)
    features = plucker_rays(target_views, target_rays, camera_turn, camera_anchor)
    embedded = jnp.dot(features, ray_weight, preferred_element_type=jnp.float32).astype(
        jnp.bfloat16
    )
    query_raw = jnp.dot(embedded, query_weight, preferred_element_type=jnp.float32)
    queries = (query_raw * rms_scale(query_raw)).astype(jnp.bfloat16)
    applied = apply_fast(queries, new_weights)
    head_terms = jnp.dot(applied, out_weight, preferred_element_type=jnp.float32)
    head_rows = pixels_true.shape[2]
    first_token = lax.axis_index("head") * head_rows
    block_sum = lax.psum_scatter(
        head_terms.astype(jnp.bfloat16), "head", scatter_dimension=0, tiled=True
    ).astype(jnp.float32)
    block_resid = (
        lax.dynamic_slice_in_dim(embedded, first_token, head_rows, 0).astype(jnp.float32)
        + block_sum
    )
    block_normed = (block_resid * rms_scale(block_resid) * norm_gain).astype(jnp.bfloat16)
    normed = lax.all_gather(block_normed, "head", axis=0, tiled=True)
    active = jax.nn.gelu(jnp.dot(normed, wide_weight, preferred_element_type=jnp.float32)).astype(
        jnp.bfloat16
    )
    block_mix = lax.psum_scatter(
        lax.dot_general(
            active, narrow_weight, contract_last, preferred_element_type=jnp.float32
        ).astype(jnp.bfloat16),
        "head",
        scatter_dimension=0,
        tiled=True,
    ).astype(jnp.float32)
    block_after = block_resid + block_mix
    after_scale = rms_scale(block_after)
    decoded_in = (block_after * after_scale * decode_gain).astype(jnp.bfloat16)
    logits = jnp.dot(decoded_in, decode_weight, preferred_element_type=jnp.float32)
    loss_scale = 1.0 / (transient.shape[-1] * math.sqrt(target_total))
    render_rows, grad_logits = pixel_loss(logits, pixels_true[0, 0], transient[0, 0], loss_scale)
    grad_decode_local = lax.dot_general(
        decoded_in, grad_logits, contract_rows, preferred_element_type=jnp.float32
    )
    grad_decoded = lax.dot_general(
        grad_logits, decode_weight, contract_last, preferred_element_type=jnp.float32
    )
    gained = grad_decoded * decode_gain
    cubed = after_scale * after_scale * after_scale
    grad_after = (
        after_scale * gained
        - block_after * cubed * jnp.mean(gained * block_after, axis=1, keepdims=True)
    ).astype(jnp.bfloat16)
    grad_narrow_local = lax.dot_general(
        lax.all_gather(grad_after, "head", axis=0, tiled=True),
        active,
        contract_rows,
        preferred_element_type=jnp.float32,
    )
    decode_heads = lax.psum(grad_decode_local.astype(jnp.bfloat16), "head").astype(jnp.float32)
    grad_decode, grad_narrow = (
        lax.psum_scatter(decode_heads, ("tok", "sub"), scatter_dimension=0, tiled=True),
        lax.psum_scatter(grad_narrow_local, ("tok", "sub"), scatter_dimension=0, tiled=True),
    )
    render = render_rows.reshape(1, 1, render_rows.shape[0], render_rows.shape[1])
    return (render, grad_decode, grad_narrow)


def solution(mesh):
    in_specs = (
        P(("groups", "tok", "sub"), None),
        P(("groups", "tok", "sub")),
        P(("groups", "tok", "sub")),
        P("groups", None),
        P("groups", None),
        P(("groups", "tok", "sub"), "head", None, None),
        P(("groups", "tok", "sub"), "head", None, None),
        P(None, "head"),
        P(None, "head"),
        P(None, "head"),
        P(None, "head"),
        P("head"),
        P("head", None, None, None),
        P("head", None),
        P(),
        P(),
        P(None, "head"),
        P(None, "head"),
        P(),
        P(),
    )
    out_specs = (
        P(("groups", "tok", "sub"), "head", None, None),
        P(("groups", "tok", "sub"), None),
        P(("groups", "tok", "sub"), "head"),
    )
    return jax.shard_map(
        on_device, mesh=mesh, in_specs=in_specs, out_specs=out_specs, check_vma=False
    )
```

profile of v0, /device:TPU:0, one launch (start us, length us, event | category | flops | bytes accessed | tf_op | source)
XLA Modules:
  0.0 213.1 jit_solution(4487902065863045844)
XLA Ops:
  7.2 1.3 copy-done
  8.6 1.6 multiply_reduce_fusion
  10.3 0.5 fusion.25
  10.8 0.5 fusion.23
  11.3 0.2 copy-done.12
  11.5 0.5 fusion.64
  12.7 0.7 fusion.3
  13.3 0.5 fusion.27
  13.8 0.6 convolution_bitcast_fusion
  14.5 0.6 convolution_bitcast_fusion.1
  15.1 0.8 convolution_bitcast_fusion.2
  15.9 1.0 pad_maximum_fusion
  17.1 0.1 select_reduce_fusion
  17.2 0.1 convert_dynamic-update-slice_fusion.2
  17.4 0.1 convert_dynamic-update-slice_fusion.1
  17.6 0.1 convert_dynamic-update-slice_fusion
  17.8 0.1 fusion.39
  17.9 0.1 fusion.40
  18.1 0.1 fusion.41
  18.2 0.3 convolution_convert_fusion.4
  18.6 0.3 multiply_reduce_fusion.4
  18.9 33.0 %reduce-scatter.6.cloned.1.call-done = f32[3,24,384]{2,1,0:T(8,128)} async-done(((f32[3,192,384]{2,1,0:T(8,128)}), f32[3,24,384]{2,1,0:T(8,128)}) %reduce-scatter.6.cloned.1.call-update) | async-done | bytes 110608 | tf_op jit(solution)/shard_map/reduce_scatter | solution.py:158
  51.9 1.0 multiply_reduce_fusion.6
  52.9 1.0 multiply_convert_fusion.10
  53.9 14.8 %all_gather.9 = bf16[3,192,384]{2,1,0:T(8,128)(2,1)S(1)} all-gather(bf16[3,24,384]{2,1,0:T(8,128)(2,1)S(1)} %multiply_convert_fusion.10), channel_id=1, replica_groups=mesh['groups'=2,'tok'=4,'head'=2,'sub'=2] {'tok','sub'}, dimensions={1}, use_global_device_ids=true | all-gather | bytes 497664 | tf_op jit(solution)/shard_map/all_gather | solution.py:164
  68.7 0.2 fusion.22
  69.0 0.4 fusion.6
  69.4 0.9 convolution_convert_fusion.3
  70.4 10.3 %reduce-scatter.8.cloned.1.call-done = bf16[96,768]{1,0:T(8,128)(2,1)} async-done(((bf16[192,768]{1,0:T(8,128)(2,1)}), bf16[96,768]{1,0:T(8,128)(2,1)}) %reduce-scatter.8.cloned.1.call-update) | async-done | bytes 147472 | tf_op jit(solution)/shard_map/reduce_scatter | solution.py:175
  80.7 1.2 multiply_reduce_fusion.3
  81.9 1.0 multiply_convert_fusion.8
  82.9 6.3 %all_gather.10 = bf16[192,768]{1,0:T(8,128)(2,1)S(1)} all-gather(bf16[96,768]{1,0:T(8,128)(2,1)S(1)} %multiply_convert_fusion.8), channel_id=1, replica_groups=mesh['groups'=2,'tok'=4,'head'=2,'sub'=2] {'head'}, dimensions={0}, use_global_device_ids=true | all-gather | bytes 442368 | tf_op jit(solution)/shard_map/all_gather | solution.py:183
  89.2 1.7 fusion.65
  90.9 1.3 convolution_convert_fusion.2
  92.4 12.0 %reduce-scatter.10.cloned.1.call-done = bf16[96,768]{1,0:T(8,128)(2,1)} async-done(((bf16[192,768]{1,0:T(8,128)(2,1)}), bf16[96,768]{1,0:T(8,128)(2,1)}) %reduce-scatter.10.cloned.1.call-update) | async-done | bytes 147472 | tf_op jit(solution)/shard_map/reduce_scatter | solution.py:187
  104.4 1.1 multiply_reduce_fusion.2
  105.5 1.0 fusion.59
  107.0 0.1 multiply_reduce_fusion.5
  107.3 1.1 convolution_convert_fusion
  108.5 25.9 %all-reduce.2.cloned.1.call-done = bf16[768,256]{1,0:T(8,128)(2,1)} async-done(((bf16[768,256]{1,0:T(8,128)(2,1)}), bf16[768,256]{1,0:T(8,128)(2,1)}) %all-reduce.2.cloned.1.call-update) | async-done | bytes 393232 | tf_op jit(solution)/shard_map/psum | solution.py:219
  134.4 1.9 convert_element_type.136
  136.4 0.4 multiply_reduce_fusion.1
  136.8 0.1 subtract_convert_fusion
  136.9 6.3 %all_gather.11 = bf16[192,768]{1,0:T(8,128)(2,1)S(1)} all-gather(bf16[96,768]{1,0:T(8,128)(2,1)S(1)} %subtract_convert_fusion), channel_id=1, replica_groups=mesh['groups'=2,'tok'=4,'head'=2,'sub'=2] {'head'}, dimensions={0}, use_global_device_ids=true | all-gather | bytes 442368 | tf_op jit(solution)/shard_map/all_gather | solution.py:214
  143.2 2.0 fusion.60
  145.2 0.6 convert_bitcast_fusion
  145.8 22.9 %reduce-scatter.12.cloned.1.call-done = f32[96,256]{1,0:T(8,128)} async-done(((f32[768,256]{1,0:T(8,128)}), f32[96,256]{1,0:T(8,128)}) %reduce-scatter.12.cloned.1.call-update) | async-done | bytes 98320 | tf_op jit(solution)/shard_map/reduce_scatter | solution.py:221
  168.7 37.5 %reduce-scatter.14.cloned.1.call-done = f32[96,768]{1,0:T(8,128)} async-done(((f32[768,768]{1,0:T(8,128)}), f32[96,768]{1,0:T(8,128)}) %reduce-scatter.14.cloned.1.call-update) | async-done | bytes 294928 | tf_op jit(solution)/shard_map/reduce_scatter | solution.py:222
  (73 shorter events, 1.5 us)
Async XLA Ops:
  7.2 1.4 copy-start
  7.2 3.1 %copy-start.3 = (bf16[1,3,192,384]{3,2,1,0:T(8,128)(2,1)S(1)}, bf16[1,3,192,384]{3,2,1,0:T(8,128)(2,1)}, u32[]{:S(2)}) copy-start(bf16[1,3,192,384]{3,2,1,0:T(8,128)(2,1)} %param.32) | copy-start | bytes 1327108
  7.2 44.7 %reduce-scatter.6.cloned.1.call-start = ((), (), s32[]{:S(2)}) async-start(), calls=%async_computation.5 | async-start | bytes 995328 | tf_op jit(solution)/shard_map/reduce_scatter | solution.py:158
  10.8 0.7 copy-start.12
  10.8 1.9 copy-start.17
  15.9 1.1 copy-start.14
  15.9 1.2 copy-start.10
  15.9 1.3 copy-start.15
  15.9 1.6 copy-start.13
  15.9 2.3 %copy-start.4 = (bf16[384,768]{1,0:T(8,128)(2,1)S(1)}, bf16[384,768]{1,0:T(8,128)(2,1)}, u32[]{:S(2)}) copy-start(bf16[384,768]{1,0:T(8,128)(2,1)} %param.34) | copy-start | bytes 1769476
  16.9 1.6 copy-start.5
  17.0 63.7 %reduce-scatter.8.cloned.1.call-start = ((), (), s32[]{:S(2)}) async-start(), calls=%async_computation.6 | async-start | bytes 442368 | tf_op jit(solution)/shard_map/reduce_scatter | solution.py:175
  53.9 15.5 %copy-start.6 = (bf16[192,768]{1,0:T(8,128)(2,1)S(1)}, bf16[192,768]{1,0:T(8,128)(2,1)}, u32[]{:S(2)}) copy-start(bf16[192,768]{1,0:T(8,128)(2,1)} %param.33) | copy-start | bytes 884740
  69.0 12.9 %copy-start.11 = (f32[768]{0:T(1024)S(1)}, f32[768]{0:T(1024)}, u32[]{:S(2)}) copy-start(f32[768]{0:T(1024)} %param.35) | copy-start | bytes 9220
  70.3 34.0 %reduce-scatter.10.cloned.1.call-start = ((), (), s32[]{:S(2)}) async-start(), calls=%async_computation.7 | async-start | bytes 442368 | tf_op jit(solution)/shard_map/reduce_scatter | solution.py:187
  80.7 10.1 %copy-start.16 = (bf16[768,768]{1,0:T(8,128)(2,1)S(1)}, bf16[768,768]{1,0:T(8,128)(2,1)}, u32[]{:S(2)}) copy-start(bf16[768,768]{1,0:T(8,128)(2,1)} %param.37) | copy-start | bytes 3538948
  90.8 1.4 copy-start.7
  90.9 13.5 %copy-start.2 = (bf16[96,768]{1,0:T(8,128)(2,1)S(1)}, bf16[96,768]{1,0:T(8,128)(2,1)}, u32[]{:S(2)}) copy-start(bf16[96,768]{1,0:T(8,128)(2,1)} %reduce-scatter.8.cloned.1.call-done) | copy-start | bytes 442372
  90.9 14.6 %copy-start.1 = (bf16[768,256]{1,0:T(8,128)(2,1)S(1)}, bf16[768,256]{1,0:T(8,128)(2,1)}, u32[]{:S(2)}) copy-start(bf16[768,256]{1,0:T(8,128)(2,1)} %param.39) | copy-start | bytes 1179652
  92.1 14.5 %copy-start.8 = (s32[1,1,96,64]{2,3,1,0:T(8,128)S(1)}, s32[1,1,96,64]{2,3,1,0:T(8,128)}, u32[]{:S(2)}) copy-start(s32[1,1,96,64]{2,3,1,0:T(8,128)} %param.26) | copy-start | bytes 73732
  92.2 42.2 %all-reduce.2.cloned.1.call-start = ((), (), s32[]{:S(2)}) async-start(), calls=%async_computation.8 | async-start | bytes 786432 | tf_op jit(solution)/shard_map/psum | solution.py:219
  105.4 1.9 copy-start.9
  108.5 60.2 %reduce-scatter.12.cloned.1.call-start = ((), (), s32[]{:S(2)}) async-start(), calls=%async_computation.9 | async-start | bytes 884736 | tf_op jit(solution)/shard_map/reduce_scatter | solution.py:221
  136.3 69.9 %reduce-scatter.14.cloned.1.call-start = ((), (), s32[]{:S(2)}) async-start(), calls=%async_computation.10 | async-start | bytes 2654208 | tf_op jit(solution)/shard_map/reduce_scatter | solution.py:222
Sparse Core Ops, SparseCore 0:
  17.1 34.7 reduce-scatter.5
  70.4 10.1 reduce-scatter.7
  92.3 12.0 reduce-scatter.9
  108.6 25.7 all-reduce.1
  137.1 31.5 reduce-scatter.11
  171.5 34.6 reduce-scatter.13
where the time goes:
time: 213 us
  waiting for transfers between devices  142 us (67%)
  blocking collectives  27.4 us (13%)
  matrix products  15.8 us (7%)
  between operations  15.4 us (7%)
  other arithmetic  9.69 us (5%)
  local copies, waits for them, and re-layouts  2.95 us (1%)
    reduce_scatter x1, waiting for transfers between devices, on_device(): lax.psum_scatter(grad_narrow_local, ('tok', 'sub'), scatter_dimension=0,...  37.5 us
    reduce_scatter x1, waiting for transfers between devices, on_device(): lax.psum_scatter(local_grads, ('tok', 'sub'), scatter_dimension=1, tiled=...  33 us
    psum x1, waiting for transfers between devices, on_device(): lax.psum(grad_decode_local.astype(jnp.bfloat16), 'head').astype(jnp.float32)  25.9 us
    reduce_scatter x1, waiting for transfers between devices, on_device(): lax.psum_scatter(decode_heads, ('tok', 'sub'), scatter_dimension=0, tiled...  22.9 us
    all_gather x1, blocking collectives, on_device(): new_weights = lax.all_gather(fresh_rows, ('tok', 'sub'), axis=1, tiled=True)  14.8 us
    reduce_scatter x1, waiting for transfers between devices, on_device(): lax.psum_scatter(lax.dot_general(active, narrow_weight, contract_last, pr...  12 us
    reduce_scatter x1, waiting for transfers between devices, on_device(): lax.psum_scatter(head_terms.astype(jnp.bfloat16), 'head', scatter_dimensi...  10.3 us
    all_gather x1, blocking collectives, on_device(): normed = lax.all_gather(block_normed, 'head', axis=0, tiled=True)  6.27 us
  transfers between devices with their start and end apart: 6, of which 6 were waited for; matrix products, arithmetic and copies ran while one was open for 2% of the time, Pallas kernels for 0%

commit v1 on v0

--- a/solution.py
+++ b/solution.py
@@ -1,8 +1,11 @@
+import functools
 import math
 
 import jax
 import jax.numpy as jnp
 from jax import lax
+from jax.experimental import pallas as pl
+from jax.experimental.pallas import tpu as pltpu
 from jax.sharding import PartitionSpec as P
 
 PATCH = 8
@@ -225,6 +228,467 @@
     return (render, grad_decode, grad_narrow)
 
 
+CHUNK_PAD = 16
+NT = (((1,), (1,)), ((), ()))
+TN = (((0,), (0,)), ((), ()))
+MESH = pl.DeviceIdType.MESH
+
+
+def dot(a, b, dims=None):
+    if dims is None:
+        dims = (((1,), (0,)), ((), ()))
+    return lax.dot_general(a, b, dims, preferred_element_type=jnp.float32)
+
+
+def dot_exact(a, b, dims):
+    return lax.dot_general(
+        a, b, dims, precision=lax.Precision.HIGHEST, preferred_element_type=jnp.float32
+    )
+
+
+def softplus(x):
+    return jnp.maximum(x, 0.0) + jnp.log1p(jnp.exp(-jnp.abs(x)))
+
+
+def gelu(x):
+    return 0.5 * x * (1.0 + jnp.tanh(0.7978845608028654 * (x + 0.044715 * (x * x * x))))
+
+
+def scene_kernel(
+    tok_n,
+    rate_scale,
+    loss_scale,
+    x_ref,
+    kw_ref,
+    vw_ref,
+    rw_ref,
+    rb_ref,
+    start_ref,
+    emb_ref,
+    q_ref,
+    truth_ref,
+    tran_ref,
+    ngain_ref,
+    dgain_ref,
+    outw_hbm,
+    wide_hbm,
+    narrow_hbm,
+    decw_hbm,
+    render_ref,
+    gdec_ref,
+    gnar_ref,
+    outw,
+    wide,
+    narrow,
+    decw,
+    gacc,
+    startf,
+    fsb,
+    fpr,
+    fps,
+    frr,
+    ag,
+    agp,
+    hs,
+    hr,
+    ns,
+    nr,
+    ms,
+    mr,
+    gs,
+    gr,
+    active,
+    gat,
+    dlf,
+    dsb,
+    dpr,
+    dps,
+    drr,
+    dx,
+    dxr,
+    gsb,
+    gpr,
+    gps,
+    grr,
+    send_sem,
+    recv_sem,
+    local_sem,
+):
+    t = lax.axis_index("tok")
+    h = lax.axis_index("head")
+    s = lax.axis_index("sub")
+    so = 1 - s
+    core = {"sub": so}
+    side = {"head": 1 - h}
+
+    loads = [
+        pltpu.make_async_copy(src, dst, local_sem.at[i])
+        for i, (src, dst) in enumerate(
+            ((outw_hbm, outw), (wide_hbm, wide), (narrow_hbm, narrow), (decw_hbm, decw))
+        )
+    ]
+    for load in loads:
+        load.start()
+
+    def chip(k):
+        return lax.rem(t + k, tok_n)
+
+    def source(k):
+        return lax.rem(t + tok_n - k, tok_n)
+
+    count = [0]
+
+    def remote(src, dst, where):
+        i = count[0]
+        count[0] += 1
+        return pltpu.make_async_remote_copy(
+            src_ref=src,
+            dst_ref=dst,
+            send_sem=send_sem.at[i],
+            recv_sem=recv_sem.at[i],
+            device_id=where,
+            device_id_type=MESH,
+        )
+
+    others = list(range(1, tok_n))
+    every = others + [0]
+
+    barrier = pltpu.get_barrier_semaphore()
+    for where in [core, side] + [{"tok": chip(k)} for k in others]:
+        pl.semaphore_signal(barrier, inc=1, device_id=where, device_id_type=MESH)
+
+    width = start_ref.shape[1]
+    depth = start_ref.shape[2]
+    gacc[...] = jnp.zeros_like(gacc)
+    step_rows = 256
+    rate_rows_w = jnp.broadcast_to(rw_ref[...].astype(jnp.float32), (128, rw_ref.shape[1])).astype(
+        jnp.bfloat16
+    )
+
+    def token_step(i, carry):
+        x = x_ref[pl.ds(pl.multiple_of(i * step_rows, step_rows), step_rows), :]
+        keys_raw = dot(x, kw_ref[...], NT)
+        keys = (keys_raw * rms_scale(keys_raw)).astype(jnp.bfloat16)
+        values = dot(x, vw_ref[...], NT).astype(jnp.bfloat16)
+        logit = dot(x, rate_rows_w, NT)[:, 0:1] + rb_ref[...]
+        rate = softplus(logit) * rate_scale
+        descent = (-rate * values.astype(jnp.float32)).astype(jnp.bfloat16)
+        pre_first = dot(keys, start_ref[0])
+        pre_third = dot(keys, start_ref[1])
+        sig = jax.nn.sigmoid(pre_first)
+        silu = pre_first * sig
+        hidden = (silu * pre_third).astype(jnp.bfloat16)
+        grad_hidden = dot(descent, start_ref[2])
+        grad_first = (grad_hidden * pre_third * (sig * (1.0 + pre_first * (1.0 - sig)))).astype(
+            jnp.bfloat16
+        )
+        grad_third = (grad_hidden * silu).astype(jnp.bfloat16)
+        gacc[0:width] += dot(keys, grad_first, TN)
+        gacc[width : 2 * width] += dot(keys, grad_third, TN)
+        gacc[2 * width : 3 * width] += dot(descent, hidden, TN)
+        return carry
+
+    lax.fori_loop(0, x_ref.shape[0] // step_rows, token_step, 0)
+    for m in range(3):
+        startf[m * width : (m + 1) * width] = start_ref[m].astype(jnp.float32)
+
+    rows = 3 * width // (2 * tok_n)
+    pad = fsb.shape[1] - rows
+
+    def padded(v):
+        return jnp.concatenate([v, jnp.zeros((pad, depth), jnp.float32)], axis=0).astype(
+            jnp.bfloat16
+        )
+
+    def fast_rows(c, sub):
+        return pl.ds(pl.multiple_of((c * 2 + sub) * rows, 8), rows)
+
+    pl.semaphore_wait(barrier, 1 + tok_n)
+
+    fast_pair = {}
+    for k in every:
+        fsb[k] = padded(gacc[fast_rows(chip(k), so)])
+        fast_pair[k] = remote(fsb.at[k], fpr.at[k], core)
+        fast_pair[k].start()
+    fast_chip = {}
+    for k in others:
+        fast_pair[k].wait_recv()
+        fps[k] = padded(gacc[fast_rows(chip(k), s)] + fpr[k][:rows].astype(jnp.float32))
+        fast_chip[k] = remote(fps.at[k], frr.at[k], {"tok": chip(k)})
+        fast_chip[k].start()
+    fast_pair[0].wait_recv()
+    gradient = gacc[fast_rows(t, s)] + fpr[0][:rows].astype(jnp.float32)
+    for k in others:
+        fast_chip[k].wait_recv()
+        gradient = gradient + frr[k][:rows].astype(jnp.float32)
+    start = startf[fast_rows(t, s)]
+    moved = start - gradient
+    restore = jnp.sqrt(jnp.mean(start * start, axis=-1, keepdims=True) + EPSILON)
+    ag[0] = padded(moved * rms_scale(moved) * restore)
+
+    gather_chip = {k: remote(ag.at[0], ag.at[k], {"tok": chip(k)}) for k in others}
+    gather_core = {k: remote(ag.at[k], agp.at[k], core) for k in every}
+    for k in others:
+        gather_chip[k].start()
+    gather_core[0].start()
+    for k in others:
+        gather_chip[k].wait_recv()
+        gather_core[k].start()
+        startf[fast_rows(source(k), s)] = ag[k][:rows].astype(jnp.float32)
+    startf[fast_rows(t, s)] = ag[0][:rows].astype(jnp.float32)
+    for k in every:
+        gather_core[k].wait_recv()
+        startf[fast_rows(source(k), so)] = agp[k][:rows].astype(jnp.float32)
+    fast = [startf[m * width : (m + 1) * width].astype(jnp.bfloat16) for m in range(3)]
+
+    loads[0].wait()
+
+    def head_term(q):
+        first = dot(q, fast[0])
+        third = dot(q, fast[1])
+        hidden = (first * jax.nn.sigmoid(first) * third).astype(jnp.bfloat16)
+        out = dot(hidden, fast[2], NT).astype(jnp.bfloat16)
+        return dot(out, outw[...])
+
+    hs[...] = head_term(q_ref[1 - h]).astype(jnp.bfloat16)
+    head_copy = remote(hs, hr, side)
+    head_copy.start()
+    own_term = head_term(q_ref[h])
+    resid = emb_ref[h].astype(jnp.float32) + own_term
+    head_copy.wait_recv()
+    resid = resid + hr[...].astype(jnp.float32)
+    ns[...] = (resid * rms_scale(resid) * ngain_ref[...]).astype(jnp.bfloat16)
+    norm_copy = remote(ns, nr, side)
+    norm_copy.start()
+
+    half = ns.shape[0]
+    loads[1].wait()
+    active[0:half] = gelu(dot(ns[...], wide[...])).astype(jnp.bfloat16)
+    loads[2].wait()
+    mixed = dot(active[0:half], narrow[...], NT)
+    norm_copy.wait_recv()
+    active[half : 2 * half] = gelu(dot(nr[...], wide[...])).astype(jnp.bfloat16)
+    ms[...] = dot(active[half : 2 * half], narrow[...], NT).astype(jnp.bfloat16)
+    mix_copy = remote(ms, mr, side)
+    mix_copy.start()
+    truth = truth_ref[...].astype(jnp.float32)
+    keep = (1 - tran_ref[...]).astype(jnp.float32).T
+    pixels = keep.shape[1]
+    spot = lax.broadcasted_iota(jnp.int32, (pixels, 3 * pixels), 1) - 3 * (
+        lax.broadcasted_iota(jnp.int32, (pixels, 3 * pixels), 0)
+    )
+    spread_out = jnp.where((spot >= 0) & (spot < 3), 1.0, 0.0).astype(jnp.float32)
+    loads[3].wait()
+    mix_copy.wait_recv()
+    after = resid + (mixed + mr[...].astype(jnp.float32))
+    after_scale = rms_scale(after)
+    decoded = (after * after_scale * dgain_ref[...]).astype(jnp.bfloat16)
+    logits = dot(decoded, decw[...])
+
+    colors = logits[:, : 3 * pixels]
+    render_ref[...] = colors.astype(jnp.bfloat16)
+    spread_logit = logits[:, 3 * pixels :]
+    spread = softplus(spread_logit) + BETA_FLOOR
+    error = colors - truth
+    squared = dot_exact(error * error, spread_out, NT)
+    inverse = 1.0 / (spread * spread)
+    weight = dot_exact(keep * inverse * loss_scale, spread_out, (((1,), (0,)), ((), ())))
+    grad_spread = (
+        keep
+        * (1.0 / spread - squared * inverse / spread)
+        * loss_scale
+        * jax.nn.sigmoid(spread_logit)
+    )
+    grad_logits = jnp.concatenate([weight * error, grad_spread], axis=1).astype(jnp.bfloat16)
+    grad_decoded = dot(grad_logits, decw[...], NT)
+    gained = grad_decoded * dgain_ref[...]
+    cubed = after_scale * after_scale * after_scale
+    gs[...] = (
+        after_scale * gained
+        - after * cubed * jnp.mean(gained * after, axis=1, keepdims=True)
+    ).astype(jnp.bfloat16)
+    grad_copy = remote(gs, gr, side)
+    grad_copy.start()
+
+    part = gdec_ref.shape[0]
+
+    def part_rows(c, sub):
+        return pl.ds(pl.multiple_of((c * 2 + sub) * part, 8), part)
+
+    dlf[...] = dot(decoded, grad_logits, TN)
+    dec_pair = {}
+    for k in every:
+        dsb[k] = dlf[part_rows(chip(k), so)].astype(jnp.bfloat16)
+        dec_pair[k] = remote(dsb.at[k], dpr.at[k], core)
+        dec_pair[k].start()
+
+    grad_copy.wait_recv()
+    both = jnp.concatenate([gs[...].astype(jnp.float32), gr[...].astype(jnp.float32)], axis=0)
+    both_t = both.T
+    for i in range(2 * tok_n):
+        gat[i] = both_t[i * part : (i + 1) * part].astype(jnp.bfloat16)
+    nar_pair = {}
+    for k in every:
+        gsb[k] = dot(gat[chip(k) * 2 + so], active[...]).astype(jnp.bfloat16)
+        nar_pair[k] = remote(gsb.at[k], gpr.at[k], core)
+        nar_pair[k].start()
+    dec_chip = {}
+    for k in others:
+        dec_pair[k].wait_recv()
+        dps[k] = (dlf[part_rows(chip(k), s)] + dpr[k].astype(jnp.float32)).astype(jnp.bfloat16)
+        dec_chip[k] = remote(dps.at[k], drr.at[k], {"tok": chip(k)})
+        dec_chip[k].start()
+    nar_chip = {}
+    for k in others:
+        mine = dot(gat[chip(k) * 2 + s], active[...])
+        nar_pair[k].wait_recv()
+        gps[k] = (mine + gpr[k].astype(jnp.float32)).astype(jnp.bfloat16)
+        nar_chip[k] = remote(gps.at[k], grr.at[k], {"tok": chip(k)})
+        nar_chip[k].start()
+    dec_pair[0].wait_recv()
+    dec_sum = dlf[part_rows(t, s)] + dpr[0].astype(jnp.float32)
+    for k in others:
+        dec_chip[k].wait_recv()
+        dec_sum = dec_sum + drr[k].astype(jnp.float32)
+    dx[...] = dec_sum
+    dec_side = remote(dx, dxr, side)
+    dec_side.start()
+    nar_pair[0].wait_recv()
+    gnar_ref[...] = dot(gat[t * 2 + s], active[...]) + gpr[0].astype(jnp.float32)
+    dec_side.wait_recv()
+    gdec_ref[...] = dec_sum + dxr[...]
+    for k in others:
+        nar_chip[k].wait_recv()
+        gnar_ref[...] += grr[k].astype(jnp.float32)
+
+    for group in (
+        fast_pair,
+        fast_chip,
+        gather_chip,
+        gather_core,
+        dec_pair,
+        nar_pair,
+        dec_chip,
+        nar_chip,
+    ):
+        for copy in group.values():
+            copy.wait_send()
+    for copy in (head_copy, norm_copy, mix_copy, grad_copy, dec_side):
+        copy.wait_send()
+
+
+def on_device_kernel(
+    in_tokens,
+    target_views,
+    target_rays,
+    camera_turn,
+    camera_anchor,
+    pixels_true,
+    transient,
+    query_weight,
+    key_weight,
+    value_weight,
+    rate_weight,
+    rate_bias,
+    fast_init,
+    out_weight,
+    ray_weight,
+    norm_gain,
+    wide_weight,
+    narrow_weight,
+    decode_gain,
+    decode_weight,
+):
+    tok_n = lax.axis_size("tok")
+    devices = tok_n * lax.axis_size("sub")
+    in_total = in_tokens.shape[0] * devices
+    target_total = target_views.shape[0] * devices
+    features = plucker_rays(target_views, target_rays, camera_turn, camera_anchor)
+    embedded = jnp.dot(features, ray_weight, preferred_element_type=jnp.float32).astype(
+        jnp.bfloat16
+    )
+    query_raw = jnp.dot(embedded, query_weight, preferred_element_type=jnp.float32)
+    queries = (query_raw * rms_scale(query_raw)).astype(jnp.bfloat16)
+    half = pixels_true.shape[2]
+    model = in_tokens.shape[1]
+    hidden = wide_weight.shape[1]
+    width, depth = fast_init.shape[2:]
+    fast_rows = -(-(3 * width // devices) // CHUNK_PAD) * CHUNK_PAD
+    part = model // devices
+    logit_n = decode_weight.shape[1]
+    vmem = pl.BlockSpec(memory_space=pltpu.VMEM)
+    anywhere = pl.BlockSpec(memory_space=pl.ANY)
+    bf16, f32 = jnp.bfloat16, jnp.float32
+    fast_buf = pltpu.VMEM((tok_n, fast_rows, depth), bf16)
+    row_buf = pltpu.VMEM((half, model), bf16)
+    dec_buf = pltpu.VMEM((tok_n, part, logit_n), bf16)
+    nar_buf = pltpu.VMEM((tok_n, part, hidden), bf16)
+    copies = 4 * tok_n + 4 * (tok_n - 1) + 5
+    render, grad_decode, grad_narrow = pl.pallas_call(
+        functools.partial(
+            scene_kernel,
+            tok_n,
+            RATE_SCALE / math.sqrt(in_total),
+            1.0 / (transient.shape[-1] * math.sqrt(target_total)),
+        ),
+        out_shape=(
+            jax.ShapeDtypeStruct((half, pixels_true.shape[3]), bf16),
+            jax.ShapeDtypeStruct((part, logit_n), f32),
+            jax.ShapeDtypeStruct((part, hidden), f32),
+        ),
+        in_specs=[vmem] * 12 + [anywhere] * 4,
+        out_specs=(vmem, vmem, vmem),
+        scratch_shapes=[
+            pltpu.VMEM(out_weight.shape, bf16),
+            pltpu.VMEM(wide_weight.shape, bf16),
+            pltpu.VMEM(narrow_weight.shape, bf16),
+            pltpu.VMEM(decode_weight.shape, bf16),
+            pltpu.VMEM((3 * width, depth), f32),
+            pltpu.VMEM((3 * width, depth), f32),
+        ]
+        + [fast_buf] * 6
+        + [row_buf] * 8
+        + [
+            pltpu.VMEM((2 * half, hidden), bf16),
+            pltpu.VMEM((devices, part, 2 * half), bf16),
+            pltpu.VMEM((model, logit_n), f32),
+        ]
+        + [dec_buf] * 4
+        + [pltpu.VMEM((part, logit_n), f32)] * 2
+        + [nar_buf] * 4
+        + [
+            pltpu.SemaphoreType.DMA((copies,)),
+            pltpu.SemaphoreType.DMA((copies,)),
+            pltpu.SemaphoreType.DMA((4,)),
+        ],
+        compiler_params=pltpu.CompilerParams(
+            collective_id=0, has_side_effects=True, vmem_limit_bytes=48 * 2**20
+        ),
+    )(
+        in_tokens,
+        key_weight.T,
+        value_weight.T,
+        rate_weight.T,
+        rate_bias.reshape(1, 1),
+        fast_init[0],
+        embedded.reshape(2, half, model),
+        queries.reshape(2, half, width),
+        pixels_true[0, 0],
+        transient[0, 0].T,
+        norm_gain.reshape(1, model),
+        decode_gain.reshape(1, model),
+        out_weight,
+        wide_weight,
+        narrow_weight,
+        decode_weight,
+    )
+    return (render[None, None], grad_decode, grad_narrow)
+
+
+def kernel_fits(mesh):
+    return mesh.shape["head"] == 2 and mesh.shape["sub"] == 2 and mesh.shape["tok"] in (2, 4)
+
+
 def solution(mesh):
     in_specs = (
         P(("groups", "tok", "sub"), None),
@@ -253,6 +717,7 @@
         P(("groups", "tok", "sub"), None),
         P(("groups", "tok", "sub"), "head"),
     )
+    body = on_device_kernel if kernel_fits(mesh) else on_device
     return jax.shard_map(
-        on_device, mesh=mesh, in_specs=in_specs, out_specs=out_specs, check_vma=False
-    )
+        body, mesh=mesh, in_specs=in_specs, out_specs=out_specs, check_vma=False
+    )

time: 213 us -> 81 us (0.38)
  waiting for transfers between devices: 142 us -> 0 us
  Pallas kernels: 0 us -> 65 us
  blocking collectives: 27.4 us -> 0 us
  matrix products: 15.8 us -> 1.66 us
  between operations: 15.4 us -> 1.54 us
  other arithmetic: 9.69 us -> 3.92 us
  local copies, waits for them, and re-layouts: 2.95 us -> 8.29 us
    reduce_scatter x5 -> x0, waiting for transfers between devices: 116 us -> none  [the longest x1 37.5 us: on_device(): lax.psum_scatter(grad_narrow_local, ('tok', 'sub'), scatter_dimension=0,...]
    pallas_call x0 -> x1, Pallas kernels: none -> 65 us  [on_device_kernel(): pl.pallas_call(functools.partial(scene_kernel, tok_n, RATE_SCALE / math.s...]
    all_gather x3 -> x0, blocking collectives: 27.4 us -> none  [the longest x1 14.8 us: on_device(): new_weights = lax.all_gather(fresh_rows, ('tok', 'sub'), axis=1, tiled=True)]
    psum x1 -> x0, waiting for transfers between devices: 25.9 us -> none  [on_device(): lax.psum(grad_decode_local.astype(jnp.bfloat16), 'head').astype(jnp.float32)]
    dot_general x20 -> x2, matrix products: 15.8 us -> 1.66 us  [the longest x1 1.32 us: on_device_kernel(): jnp.dot(embedded, query_weight, preferred_element_type=jnp.float32)]
    unnamed x37 -> x25, local copies, waits for them, and re-layouts: 1.71 us -> 6.9 us
    convert_element_type x5 -> x1, other arithmetic: 4.14 us -> 0.1 us  [on_device_kernel(): queries = (query_raw * rms_scale(query_raw)).astype(jnp.bfloat16)]
    reduce_sum x4 -> x0, other arithmetic: 3.33 us -> none  [the longest x3 3.23 us: rms_scale(): jnp.mean(vector * vector, axis=-1, keepdims=True) + EPSILON]
  transfers between devices with their start and end apart: 6 -> 0, of which waited for: 6 -> 0; matrix products, arithmetic and copies ran while one was open for 2% -> 0% of each run, Pallas kernels for 0% -> 0%
where the time goes in v1:
time: 81 us; the launch traced here: 80.4 us
  Pallas kernels  65 us (80%)
  local copies, waits for them, and re-layouts  8.29 us (10%)
  other arithmetic  3.92 us (5%)
  matrix products  1.66 us (2%)
  between operations  1.54 us (2%)
    pallas_call x1, Pallas kernels, on_device_kernel(): pl.pallas_call(functools.partial(scene_kernel, tok_n, RATE_SCALE / math.s...  65 us
    unnamed x25, local copies, waits for them, and re-layouts  6.9 us

profile of v1, /device:TPU:0, one launch (start us, length us, event | category | flops | bytes accessed | tf_op | source)
XLA Modules:
  0.0 80.4 jit_solution(7459423610418188383)
XLA Ops:
  0.6 0.0 copy-start
  1.4 0.7 fusion.6
  2.1 0.7 reshape.123.ngain_ref
  2.7 0.7 reshape.124.dgain_ref
  3.4 0.7 iota_compare_fusion
  4.1 0.8 select_reduce_fusion.1
  4.9 0.8 %select_reduce_fusion = f32[192,9]{0,1:T(8,128)S(1)} fusion(f32[32,9]{0,1:T(8,128)} %param.23, pred[192,32]{0,1:T(8,128)(4,1)S(1)} %iota_compare_fusion), kind=kLoop, calls=%fused_computation.1 | loop fusion | flops 108864 | bytes 14208 | tf_op jit(solution)/shard_map/reduce_sum | solution.py:32
  5.8 0.0 copy-start.8
  5.8 0.1 convert_dynamic-update-slice_fusion.2
  5.9 0.0 copy-start.9
  5.9 0.0 copy-start.10
  5.9 0.1 convert_dynamic-update-slice_fusion.1
  6.1 0.0 copy-start.1
  6.1 0.0 copy-start.2
  6.1 0.1 convert_dynamic-update-slice_fusion
  6.2 0.1 fusion.3
  6.4 0.1 fusion.4
  6.5 0.1 fusion.5
  6.7 0.0 copy-done
  6.7 0.3 convolution_convert_fusion
  7.0 1.3 %multiply_reduce_fusion = (f32[192]{0:T(256)S(1)}, f32[192,192]{1,0:T(8,128)S(1)}) fusion(bf16[192,768]{1,0:T(8,128)(2,1)S(1)} %convolution_convert_fusion, bf16[768,192]{0,1:T(8,128)(2,1)} %param.27), kind=kOutput, calls=%fused_computation.3 | convolution fusion | flops 56696640 | bytes 738048 | tf_op jit(solution)/shard_map/dot_general | solution.py:610
  8.4 0.1 multiply_convert_fusion
  8.5 0.0 copy-done.8
  8.5 0.0 copy-done.9
  8.5 0.0 copy-done.10
  8.5 0.0 copy-done.1
  8.5 0.0 copy-done.2
  8.5 0.0 copy-start.3
  8.5 1.0 %copy-done.3 = bf16[1,3,192,384]{3,2,1,0:T(8,128)(2,1)S(1)} copy-done((bf16[1,3,192,384]{3,2,1,0:T(8,128)(2,1)S(1)}, bf16[1,3,192,384]{3,2,1,0:T(8,128)(2,1)}, u32[]{:S(2)}) %copy-start.3) | copy-done | bytes 442392
  9.5 0.0 copy-start.4
  9.5 1.0 %copy-done.4 = bf16[768,256]{1,0:T(8,128)(2,1)S(1)} copy-done((bf16[768,256]{1,0:T(8,128)(2,1)S(1)}, bf16[768,256]{1,0:T(8,128)(2,1)}, u32[]{:S(2)}) %copy-start.4) | copy-done | bytes 393240
  10.5 0.0 copy-start.5
  10.5 1.0 %copy-done.5 = bf16[768,192]{0,1:T(8,128)(2,1)S(1)} copy-done((bf16[768,192]{0,1:T(8,128)(2,1)S(1)}, bf16[768,192]{0,1:T(8,128)(2,1)}, u32[]{:S(2)}) %copy-start.5) | copy-done | bytes 294936
  11.5 0.0 copy-start.6
  11.5 1.0 %copy-done.6 = bf16[768,192]{0,1:T(8,128)(2,1)S(1)} copy-done((bf16[768,192]{0,1:T(8,128)(2,1)S(1)}, bf16[768,192]{0,1:T(8,128)(2,1)}, u32[]{:S(2)}) %copy-start.6) | copy-done | bytes 294936
  12.5 0.0 copy-start.7
  12.5 1.0 %copy-done.7 = bf16[192,768]{1,0:T(8,128)(2,1)S(1)} copy-done((bf16[192,768]{1,0:T(8,128)(2,1)S(1)}, bf16[192,768]{1,0:T(8,128)(2,1)}, u32[]{:S(2)}) %copy-start.7) | copy-done | bytes 294936
  13.4 65.0 %shard_map.211 = (bf16[96,192]{1,0:T(8,128)(2,1)S(1)}, f32[96,256]{1,0:T(8,128)S(1)}, f32[96,768]{1,0:T(8,128)S(1)}) custom-call(bf16[1024,768]{1,0:T(8,128)(2,1)} %x_ref.1, bf16[192,768]{1,0:T(8,128)(2,1)S(1)} %bitcast.32, bf16[192,768]{1,0:T(8,128)(2,1)S(1)} %bitcast.33, bf16[1,768]{1,0:T(2,128)(2,1)S(1)} %bitcast.37, f32[1,1]{1,0:T(1,128)} %bitcast.28.rb_ref, ...), custom_call_target="tpu_custom_call" | custom-call | tf_op jit(solution)/shard_map/pallas_call | solution.py:627
  78.5 0.6 copy.36
  79.1 0.6 copy.37
  79.7 0.7 copy.38
  (4 shorter events, 0.0 us)
Async XLA Ops:
  0.6 6.0 %copy-start = (bf16[384,768]{1,0:T(8,128)(2,1)S(1)}, bf16[384,768]{1,0:T(8,128)(2,1)}, u32[]{:S(2)}) copy-start(bf16[384,768]{1,0:T(8,128)(2,1)} %param.34) | copy-start | bytes 1769476
  5.8 2.7 %copy-start.8 = (bf16[1,1,96,192]{3,2,1,0:T(8,128)(2,1)S(1)}, bf16[1,1,96,192]{3,2,1,0:T(8,128)(2,1)}, u32[]{:S(2)}) copy-start(bf16[1,1,96,192]{3,2,1,0:T(8,128)(2,1)} %param.25) | copy-start | bytes 110596
  5.9 2.6 %copy-start.9 = (s32[1,1,96,64]{2,3,1,0:T(8,128)S(1)}, s32[1,1,96,64]{2,3,1,0:T(8,128)}, u32[]{:S(2)}) copy-start(s32[1,1,96,64]{2,3,1,0:T(8,128)} %param.26) | copy-start | bytes 73732
  5.9 2.6 %copy-start.10 = (bf16[768,1]{0,1:T(2,128)(2,1)S(1)}, bf16[768,1]{0,1:T(2,128)(2,1)}, u32[]{:S(2)}) copy-start(bf16[768,1]{0,1:T(2,128)(2,1)} %param.30) | copy-start | bytes 4612
  6.1 2.4 %copy-start.1 = (bf16[768,768]{1,0:T(8,128)(2,1)S(1)}, bf16[768,768]{1,0:T(8,128)(2,1)}, u32[]{:S(2)}) copy-start(bf16[768,768]{1,0:T(8,128)(2,1)} %wide_hbm.1) | copy-start | bytes 3538948
  6.1 2.4 %copy-start.2 = (bf16[768,768]{1,0:T(8,128)(2,1)S(1)}, bf16[768,768]{1,0:T(8,128)(2,1)}, u32[]{:S(2)}) copy-start(bf16[768,768]{1,0:T(8,128)(2,1)} %narrow_hbm.1) | copy-start | bytes 3538948
  8.5 1.0 %copy-start.3 = (bf16[1,3,192,384]{3,2,1,0:T(8,128)(2,1)S(1)}, bf16[1,3,192,384]{3,2,1,0:T(8,128)(2,1)}, u32[]{:S(2)}) copy-start(bf16[1,3,192,384]{3,2,1,0:T(8,128)(2,1)} %param.32) | copy-start | bytes 1327108
  9.5 1.0 %copy-start.4 = (bf16[768,256]{1,0:T(8,128)(2,1)S(1)}, bf16[768,256]{1,0:T(8,128)(2,1)}, u32[]{:S(2)}) copy-start(bf16[768,256]{1,0:T(8,128)(2,1)} %decw_hbm.1) | copy-start | bytes 1179652
  10.5 1.0 %copy-start.5 = (bf16[768,192]{0,1:T(8,128)(2,1)S(1)}, bf16[768,192]{0,1:T(8,128)(2,1)}, u32[]{:S(2)}) copy-start(bf16[768,192]{0,1:T(8,128)(2,1)} %param.28) | copy-start | bytes 884740
  11.5 1.0 %copy-start.6 = (bf16[768,192]{0,1:T(8,128)(2,1)S(1)}, bf16[768,192]{0,1:T(8,128)(2,1)}, u32[]{:S(2)}) copy-start(bf16[768,192]{0,1:T(8,128)(2,1)} %param.29) | copy-start | bytes 884740
  12.5 1.0 %copy-start.7 = (bf16[192,768]{1,0:T(8,128)(2,1)S(1)}, bf16[192,768]{1,0:T(8,128)(2,1)}, u32[]{:S(2)}) copy-start(bf16[192,768]{1,0:T(8,128)(2,1)} %outw_hbm.1) | copy-start | bytes 884740

commit v2 on v1

--- a/solution.py
+++ b/solution.py
@@ -258,18 +258,22 @@
     tok_n,
     rate_scale,
     loss_scale,
-    x_ref,
-    kw_ref,
-    vw_ref,
+    rb_ref,
+    views_ref,
+    rays_ref,
+    turn_ref,
+    anchor_ref,
     rw_ref,
-    rb_ref,
-    start_ref,
-    emb_ref,
-    q_ref,
     truth_ref,
     tran_ref,
     ngain_ref,
     dgain_ref,
+    x_hbm,
+    kw_hbm,
+    vw_hbm,
+    fast_hbm,
+    ray_hbm,
+    qw_hbm,
     outw_hbm,
     wide_hbm,
     narrow_hbm,
@@ -277,6 +281,18 @@
     render_ref,
     gdec_ref,
     gnar_ref,
+    x_ref,
+    kw_ref,
+    vw_ref,
+    start_ref,
+    ray_ref,
+    qw_ref,
+    emb_ref,
+    q_ref,
+    outw_side,
+    wide_side,
+    narrow_side,
+    act_side,
     outw,
     wide,
     narrow,
@@ -291,10 +307,6 @@
     agp,
     hs,
     hr,
-    ns,
-    nr,
-    ms,
-    mr,
     gs,
     gr,
     active,
@@ -321,14 +333,28 @@
     core = {"sub": so}
     side = {"head": 1 - h}
 
+    step_rows = 256
+    steps = x_hbm.shape[0] // step_rows
+    pairs = [(kw_hbm, kw_ref), (fast_hbm, start_ref), (vw_hbm, vw_ref)]
+    pairs += [
+        (x_hbm.at[pl.ds(i * step_rows, step_rows)], x_ref.at[pl.ds(i * step_rows, step_rows)])
+        for i in range(steps)
+    ]
+    first_loads = len(pairs)
+    pairs += [
+        (ray_hbm, ray_ref),
+        (qw_hbm, qw_ref),
+        (outw_hbm, outw),
+        (wide_hbm, wide),
+        (narrow_hbm, narrow),
+        (decw_hbm, decw),
+    ]
     loads = [
-        pltpu.make_async_copy(src, dst, local_sem.at[i])
-        for i, (src, dst) in enumerate(
-            ((outw_hbm, outw), (wide_hbm, wide), (narrow_hbm, narrow), (decw_hbm, decw))
-        )
+        pltpu.make_async_copy(src, dst, local_sem.at[i]) for i, (src, dst) in enumerate(pairs)
     ]
     for load in loads:
         load.start()
+    ray_load, qw_load, outw_load, wide_load, narrow_load, decw_load = loads[first_loads:]
 
     def chip(k):
         return lax.rem(t + k, tok_n)
@@ -357,10 +383,26 @@
     for where in [core, side] + [{"tok": chip(k)} for k in others]:
         pl.semaphore_signal(barrier, inc=1, device_id=where, device_id_type=MESH)
 
+    pl.semaphore_wait(barrier, 1 + tok_n)
+
+    def half_rows(ref):
+        n = ref.shape[0] // 2
+        return ref.at[pl.ds(pl.multiple_of(s * n, n), n)]
+
+    def fetch(hbm, target):
+        over = remote(half_rows(hbm), half_rows(target), side)
+        share = remote(half_rows(target), half_rows(target), core)
+        return over, share
+
+    outw_over, outw_share = fetch(outw_hbm, outw_side)
+    wide_over, wide_share = fetch(wide_hbm, wide_side)
+    narrow_over, narrow_share = fetch(narrow_hbm, narrow_side)
+    outw_over.start()
+    wide_over.start()
+
     width = start_ref.shape[1]
     depth = start_ref.shape[2]
     gacc[...] = jnp.zeros_like(gacc)
-    step_rows = 256
     rate_rows_w = jnp.broadcast_to(rw_ref[...].astype(jnp.float32), (128, rw_ref.shape[1])).astype(
         jnp.bfloat16
     )
@@ -370,7 +412,7 @@
         keys_raw = dot(x, kw_ref[...], NT)
         keys = (keys_raw * rms_scale(keys_raw)).astype(jnp.bfloat16)
         values = dot(x, vw_ref[...], NT).astype(jnp.bfloat16)
-        logit = dot(x, rate_rows_w, NT)[:, 0:1] + rb_ref[...]
+        logit = dot(x, rate_rows_w, NT)[:, 0:1] + rb_ref[0]
         rate = softplus(logit) * rate_scale
         descent = (-rate * values.astype(jnp.float32)).astype(jnp.bfloat16)
         pre_first = dot(keys, start_ref[0])
@@ -388,7 +430,9 @@
         gacc[2 * width : 3 * width] += dot(descent, hidden, TN)
         return carry
 
-    lax.fori_loop(0, x_ref.shape[0] // step_rows, token_step, 0)
+    for load in loads[:first_loads]:
+        load.wait()
+    lax.fori_loop(0, steps, token_step, 0)
     for m in range(3):
         startf[m * width : (m + 1) * width] = start_ref[m].astype(jnp.float32)
 
@@ -403,7 +447,9 @@
     def fast_rows(c, sub):
         return pl.ds(pl.multiple_of((c * 2 + sub) * rows, 8), rows)
 
-    pl.semaphore_wait(barrier, 1 + tok_n)
+    outw_over.wait_recv()
+    outw_share.start()
+    narrow_over.start()
 
     fast_pair = {}
     for k in every:
@@ -416,6 +462,63 @@
         fps[k] = padded(gacc[fast_rows(chip(k), s)] + fpr[k][:rows].astype(jnp.float32))
         fast_chip[k] = remote(fps.at[k], frr.at[k], {"tok": chip(k)})
         fast_chip[k].start()
+
+    views = views_ref[...][None, :]
+    rays = rays_ref[...][None, :]
+    cameras = turn_ref.shape[1]
+    targets = views.shape[1]
+    chosen = jnp.where(
+        lax.broadcasted_iota(jnp.int32, (cameras, targets), 0) == views, 1.0, 0.0
+    ).astype(jnp.float32)
+    plain = (((1,), (0,)), ((), ()))
+    across = IMG // PATCH
+    table = jnp.concatenate(
+        [
+            dot_exact(turn_ref[...], chosen, plain),
+            dot_exact(anchor_ref[...], chosen, plain),
+            jnp.bitwise_and(rays, across - 1).astype(jnp.float32),
+            lax.shift_right_logical(rays, across.bit_length() - 1).astype(jnp.float32),
+            jnp.zeros((2, targets), jnp.float32),
+        ],
+        axis=0,
+    ).T
+
+    def entry(i):
+        return table[:, i : i + 1]
+
+    spots = lax.broadcasted_iota(jnp.int32, (1, PATCH * PATCH), 1)
+    spot_x = jnp.bitwise_and(spots, PATCH - 1).astype(jnp.float32)
+    spot_y = lax.shift_right_logical(spots, PATCH.bit_length() - 1).astype(jnp.float32)
+    camera_x = (entry(12) * PATCH + spot_x + 0.5 - 0.5 * IMG) / IMG
+    camera_y = (entry(13) * PATCH + spot_y + 0.5 - 0.5 * IMG) / IMG
+    dir_x = (1.0 + entry(0)) * camera_x + entry(1) * camera_y + entry(2)
+    dir_y = entry(3) * camera_x + (1.0 + entry(4)) * camera_y + entry(5)
+    dir_z = entry(6) * camera_x + entry(7) * camera_y + (1.0 + entry(8))
+    norm_inv = lax.rsqrt(dir_x * dir_x + dir_y * dir_y + dir_z * dir_z)
+    dir_x = dir_x * norm_inv
+    dir_y = dir_y * norm_inv
+    dir_z = dir_z * norm_inv
+    features = jnp.concatenate(
+        [
+            dir_x,
+            dir_y,
+            dir_z,
+            entry(10) * dir_z - entry(11) * dir_y,
+            entry(11) * dir_x - entry(9) * dir_z,
+            entry(9) * dir_y - entry(10) * dir_x,
+        ],
+        axis=1,
+    ).astype(jnp.bfloat16)
+    half = emb_ref.shape[1]
+    ray_load.wait()
+    qw_load.wait()
+    embedded = dot(features, ray_ref[...]).astype(jnp.bfloat16)
+    query_raw = dot(embedded, qw_ref[...], NT)
+    queries = (query_raw * rms_scale(query_raw)).astype(jnp.bfloat16)
+    for i in range(2):
+        emb_ref[i] = embedded[i * half : (i + 1) * half]
+        q_ref[i] = queries[i * half : (i + 1) * half]
+
     fast_pair[0].wait_recv()
     gradient = gacc[fast_rows(t, s)] + fpr[0][:rows].astype(jnp.float32)
     for k in others:
@@ -431,6 +534,8 @@
     for k in others:
         gather_chip[k].start()
     gather_core[0].start()
+    wide_over.wait_recv()
+    wide_share.start()
     for k in others:
         gather_chip[k].wait_recv()
         gather_core[k].start()
@@ -441,36 +546,35 @@
         startf[fast_rows(source(k), so)] = agp[k][:rows].astype(jnp.float32)
     fast = [startf[m * width : (m + 1) * width].astype(jnp.bfloat16) for m in range(3)]
 
-    loads[0].wait()
-
-    def head_term(q):
+    def head_out(q):
         first = dot(q, fast[0])
         third = dot(q, fast[1])
         hidden = (first * jax.nn.sigmoid(first) * third).astype(jnp.bfloat16)
-        out = dot(hidden, fast[2], NT).astype(jnp.bfloat16)
-        return dot(out, outw[...])
-
-    hs[...] = head_term(q_ref[1 - h]).astype(jnp.bfloat16)
+        return dot(hidden, fast[2], NT).astype(jnp.bfloat16)
+
+    hs[...] = head_out(q_ref[1 - h])
     head_copy = remote(hs, hr, side)
     head_copy.start()
-    own_term = head_term(q_ref[h])
-    resid = emb_ref[h].astype(jnp.float32) + own_term
+    own_out = head_out(q_ref[h])
+    outw_load.wait()
+    outw_share.wait_recv()
+    resid = emb_ref[h].astype(jnp.float32) + dot(own_out, outw[...])
+    narrow_over.wait_recv()
+    narrow_share.start()
     head_copy.wait_recv()
-    resid = resid + hr[...].astype(jnp.float32)
-    ns[...] = (resid * rms_scale(resid) * ngain_ref[...]).astype(jnp.bfloat16)
-    norm_copy = remote(ns, nr, side)
-    norm_copy.start()
-
-    half = ns.shape[0]
-    loads[1].wait()
-    active[0:half] = gelu(dot(ns[...], wide[...])).astype(jnp.bfloat16)
-    loads[2].wait()
+    resid = resid + dot(hr[...], outw_side[...])
+    normed = (resid * rms_scale(resid) * ngain_ref[...][None, :]).astype(jnp.bfloat16)
+
+    wide_load.wait()
+    wide_share.wait_recv()
+    act_side[...] = gelu(dot(normed, wide_side[...])).astype(jnp.bfloat16)
+    act_copy = remote(act_side, active.at[pl.ds(half, half)], side)
+    act_copy.start()
+    active[0:half] = gelu(dot(normed, wide[...])).astype(jnp.bfloat16)
+    narrow_load.wait()
     mixed = dot(active[0:half], narrow[...], NT)
-    norm_copy.wait_recv()
-    active[half : 2 * half] = gelu(dot(nr[...], wide[...])).astype(jnp.bfloat16)
-    ms[...] = dot(active[half : 2 * half], narrow[...], NT).astype(jnp.bfloat16)
-    mix_copy = remote(ms, mr, side)
-    mix_copy.start()
+    narrow_share.wait_recv()
+    after = resid + (mixed + dot(act_side[...], narrow_side[...], NT))
     truth = truth_ref[...].astype(jnp.float32)
     keep = (1 - tran_ref[...]).astype(jnp.float32).T
     pixels = keep.shape[1]
@@ -478,11 +582,9 @@
         lax.broadcasted_iota(jnp.int32, (pixels, 3 * pixels), 0)
     )
     spread_out = jnp.where((spot >= 0) & (spot < 3), 1.0, 0.0).astype(jnp.float32)
-    loads[3].wait()
-    mix_copy.wait_recv()
-    after = resid + (mixed + mr[...].astype(jnp.float32))
+    decw_load.wait()
     after_scale = rms_scale(after)
-    decoded = (after * after_scale * dgain_ref[...]).astype(jnp.bfloat16)
+    decoded = (after * after_scale * dgain_ref[...][None, :]).astype(jnp.bfloat16)
     logits = dot(decoded, decw[...])
 
     colors = logits[:, : 3 * pixels]
@@ -501,7 +603,7 @@
     )
     grad_logits = jnp.concatenate([weight * error, grad_spread], axis=1).astype(jnp.bfloat16)
     grad_decoded = dot(grad_logits, decw[...], NT)
-    gained = grad_decoded * dgain_ref[...]
+    gained = grad_decoded * dgain_ref[...][None, :]
     cubed = after_scale * after_scale * after_scale
     gs[...] = (
         after_scale * gained
@@ -523,6 +625,7 @@
         dec_pair[k].start()
 
     grad_copy.wait_recv()
+    act_copy.wait_recv()
     both = jnp.concatenate([gs[...].astype(jnp.float32), gr[...].astype(jnp.float32)], axis=0)
     both_t = both.T
     for i in range(2 * tok_n):
@@ -573,7 +676,18 @@
     ):
         for copy in group.values():
             copy.wait_send()
-    for copy in (head_copy, norm_copy, mix_copy, grad_copy, dec_side):
+    for copy in (
+        head_copy,
+        act_copy,
+        grad_copy,
+        dec_side,
+        outw_over,
+        outw_share,
+        wide_over,
+        wide_share,
+        narrow_over,
+        narrow_share,
+    ):
         copy.wait_send()
 
 
@@ -603,12 +717,6 @@
     devices = tok_n * lax.axis_size("sub")
     in_total = in_tokens.shape[0] * devices
     target_total = target_views.shape[0] * devices
-    features = plucker_rays(target_views, target_rays, camera_turn, camera_anchor)
-    embedded = jnp.dot(features, ray_weight, preferred_element_type=jnp.float32).astype(
-        jnp.bfloat16
-    )
-    query_raw = jnp.dot(embedded, query_weight, preferred_element_type=jnp.float32)
-    queries = (query_raw * rms_scale(query_raw)).astype(jnp.bfloat16)
     half = pixels_true.shape[2]
     model = in_tokens.shape[1]
     hidden = wide_weight.shape[1]
@@ -623,7 +731,7 @@
     row_buf = pltpu.VMEM((half, model), bf16)
     dec_buf = pltpu.VMEM((tok_n, part, logit_n), bf16)
     nar_buf = pltpu.VMEM((tok_n, part, hidden), bf16)
-    copies = 4 * tok_n + 4 * (tok_n - 1) + 5
+    copies = 4 * tok_n + 4 * (tok_n - 1) + 10
     render, grad_decode, grad_narrow = pl.pallas_call(
         functools.partial(
             scene_kernel,
@@ -636,9 +744,21 @@
             jax.ShapeDtypeStruct((part, logit_n), f32),
             jax.ShapeDtypeStruct((part, hidden), f32),
         ),
-        in_specs=[vmem] * 12 + [anywhere] * 4,
+        in_specs=[pl.BlockSpec(memory_space=pltpu.SMEM)] + [vmem] * 9 + [anywhere] * 10,
         out_specs=(vmem, vmem, vmem),
         scratch_shapes=[
+            pltpu.VMEM(in_tokens.shape, bf16),
+            pltpu.VMEM((width, model), bf16),
+            pltpu.VMEM((width, model), bf16),
+            pltpu.VMEM((3, width, depth), bf16),
+            pltpu.VMEM(ray_weight.shape, bf16),
+            pltpu.VMEM((width, model), bf16),
+            pltpu.VMEM((2, half, model), bf16),
+            pltpu.VMEM((2, half, width), bf16),
+            pltpu.VMEM(out_weight.shape, bf16),
+            pltpu.VMEM(wide_weight.shape, bf16),
+            pltpu.VMEM(narrow_weight.shape, bf16),
+            pltpu.VMEM((half, hidden), bf16),
             pltpu.VMEM(out_weight.shape, bf16),
             pltpu.VMEM(wide_weight.shape, bf16),
             pltpu.VMEM(narrow_weight.shape, bf16),
@@ -647,7 +767,8 @@
             pltpu.VMEM((3 * width, depth), f32),
         ]
         + [fast_buf] * 6
-        + [row_buf] * 8
+        + [pltpu.VMEM((half, width), bf16)] * 2
+        + [row_buf] * 2
         + [
             pltpu.VMEM((2 * half, hidden), bf16),
             pltpu.VMEM((devices, part, 2 * half), bf16),
@@ -659,24 +780,28 @@
         + [
             pltpu.SemaphoreType.DMA((copies,)),
             pltpu.SemaphoreType.DMA((copies,)),
-            pltpu.SemaphoreType.DMA((4,)),
+            pltpu.SemaphoreType.DMA((9 + in_tokens.shape[0] // 256,)),
         ],
         compiler_params=pltpu.CompilerParams(
-            collective_id=0, has_side_effects=True, vmem_limit_bytes=48 * 2**20
+            collective_id=0, has_side_effects=True, vmem_limit_bytes=60 * 2**20
         ),
     )(
+        rate_bias,
+        target_views,
+        target_rays,
+        camera_turn.T,
+        camera_anchor.T,
+        rate_weight.T,
+        pixels_true[0, 0],
+        transient[0, 0].T,
+        norm_gain,
+        decode_gain,
         in_tokens,
         key_weight.T,
         value_weight.T,
-        rate_weight.T,
-        rate_bias.reshape(1, 1),
         fast_init[0],
-        embedded.reshape(2, half, model),
-        queries.reshape(2, half, width),
-        pixels_true[0, 0],
-        transient[0, 0].T,
-        norm_gain.reshape(1, model),
-        decode_gain.reshape(1, model),
+        ray_weight,
+        query_weight.T,
         out_weight,
         wide_weight,
         narrow_weight,

time: 81 us -> 70.4 us (0.87)
  other arithmetic: 3.92 us -> 0 us
  local copies, waits for them, and re-layouts: 8.29 us -> 4.65 us
  matrix products: 1.66 us -> 0 us
  Pallas kernels: 65 us -> 64.1 us
    unnamed x25 -> x3, local copies, waits for them, and re-layouts: 6.9 us -> 4.65 us
    dot_general x2 -> x0, matrix products: 1.66 us -> none  [the longest x1 1.32 us: on_device_kernel(): jnp.dot(embedded, query_weight, preferred_element_type=jnp.float32)]
    reduce_sum x2 -> x0, other arithmetic: 1.59 us -> none  [the longest x1 0.82 us: plucker_rays(): jnp.sum(jnp.where(one_hot[:, :, None], camera_turn[None, :, :], 0.0), axi...]
    reshape x2 -> x0, local copies, waits for them, and re-layouts: 1.38 us -> none  [the longest x1 0.69 us: on_device_kernel(): norm_gain.reshape(1, model)]
    pallas_call x1, Pallas kernels: 65 us -> 64.1 us  [on_device_kernel(): pl.pallas_call(functools.partial(scene_kernel, tok_n, RATE_SCALE / math.s...]
where the time goes in v2:
time: 70.4 us; the launch traced here: 70.1 us
  Pallas kernels  64.1 us (91%)
  local copies, waits for them, and re-layouts  4.65 us (7%)
  between operations  1.29 us (2%)
    pallas_call x1, Pallas kernels, on_device_kernel(): pl.pallas_call(functools.partial(scene_kernel, tok_n, RATE_SCALE / math.s...  64.1 us
    unnamed x3, local copies, waits for them, and re-layouts  4.65 us

profile of v2, /device:TPU:0, one launch (start us, length us, event | category | flops | bytes accessed | tf_op | source)
XLA Modules:
  0.0 70.1 jit_solution(12583857800095116499)
XLA Ops:
  1.3 64.1 %shard_map.211 = (bf16[96,192]{1,0:T(8,128)(2,1)}, f32[96,256]{1,0:T(8,128)}, f32[96,768]{1,0:T(8,128)}) custom-call(f32[1]{0:T(128)S(6)} %copy.26.rb_ref, s32[192]{0:T(256)} %views_ref.1, s32[192]{0:T(256)} %rays_ref.1, f32[9,32]{1,0:T(8,128)} %bitcast.19, f32[3,32]{1,0:T(4,128)} %bitcast.21, bf16[1,768]{1,0:T(2,128)(2,1)} %bitcast.20, ...), custom_call_target="tpu_custom_call" | custom-call | tf_op jit(solution)/shard_map/pallas_call | solution.py:735
  65.4 1.4 %copy.27 = bf16[1,1,96,192]{3,2,1,0:T(8,128)(2,1)} copy(bf16[1,1,96,192]{3,2,1,0:T(8,128)(2,1)} %bitcast.17) | data formatting | bytes 73728
  66.8 1.5 %copy.28 = f32[96,256]{1,0:T(8,128)} copy(f32[96,256]{1,0:T(8,128)} %get-tuple-element.13) | data formatting | bytes 196608
  68.4 1.7 %copy.29 = f32[96,768]{1,0:T(8,128)} copy(f32[96,768]{1,0:T(8,128)} %get-tuple-element.14) | data formatting | bytes 589824

commit v3 on v2

--- a/solution.py
+++ b/solution.py
@@ -328,12 +328,14 @@
 ):
     t = lax.axis_index("tok")
     h = lax.axis_index("head")
+    g = lax.axis_index("groups")
     s = lax.axis_index("sub")
     so = 1 - s
     core = {"sub": so}
     side = {"head": 1 - h}
-
-    step_rows = 256
+    twin = {"groups": 1 - g}
+
+    step_rows = 512
     steps = x_hbm.shape[0] // step_rows
     pairs = [(kw_hbm, kw_ref), (fast_hbm, start_ref), (vw_hbm, vw_ref)]
     pairs += [
@@ -352,7 +354,7 @@
     loads = [
         pltpu.make_async_copy(src, dst, local_sem.at[i]) for i, (src, dst) in enumerate(pairs)
     ]
-    for load in loads:
+    for load in loads[:first_loads]:
         load.start()
     ray_load, qw_load, outw_load, wide_load, narrow_load, decw_load = loads[first_loads:]
 
@@ -380,25 +382,33 @@
     every = others + [0]
 
     barrier = pltpu.get_barrier_semaphore()
-    for where in [core, side] + [{"tok": chip(k)} for k in others]:
+    for where in [core, side, twin] + [{"tok": chip(k)} for k in others]:
         pl.semaphore_signal(barrier, inc=1, device_id=where, device_id_type=MESH)
 
-    pl.semaphore_wait(barrier, 1 + tok_n)
-
-    def half_rows(ref):
-        n = ref.shape[0] // 2
-        return ref.at[pl.ds(pl.multiple_of(s * n, n), n)]
+    for load in loads[:first_loads]:
+        load.wait()
+    for load in loads[first_loads:]:
+        load.start()
+    pl.semaphore_wait(barrier, 2 + tok_n)
+
+    def quarter(ref, g_, s_):
+        n = ref.shape[0] // 4
+        return ref.at[pl.ds(pl.multiple_of((2 * g_ + s_) * n, n), n)]
 
     def fetch(hbm, target):
-        over = remote(half_rows(hbm), half_rows(target), side)
-        share = remote(half_rows(target), half_rows(target), core)
-        return over, share
-
-    outw_over, outw_share = fetch(outw_hbm, outw_side)
-    wide_over, wide_share = fetch(wide_hbm, wide_side)
-    narrow_over, narrow_share = fetch(narrow_hbm, narrow_side)
-    outw_over.start()
-    wide_over.start()
+        mine, twins = quarter(target, g, s), quarter(target, 1 - g, s)
+        return (
+            remote(quarter(hbm, g, s), mine, side),
+            remote(mine, mine, twin),
+            remote(mine, mine, core),
+            remote(twins, twins, core),
+        )
+
+    outw_side_in, outw_twin, outw_core, outw_core2 = fetch(outw_hbm, outw_side)
+    wide_side_in, wide_twin, wide_core, wide_core2 = fetch(wide_hbm, wide_side)
+    narrow_side_in, narrow_twin, narrow_core, narrow_core2 = fetch(narrow_hbm, narrow_side)
+    outw_side_in.start()
+    wide_side_in.start()
 
     width = start_ref.shape[1]
     depth = start_ref.shape[2]
@@ -430,8 +440,6 @@
         gacc[2 * width : 3 * width] += dot(descent, hidden, TN)
         return carry
 
-    for load in loads[:first_loads]:
-        load.wait()
     lax.fori_loop(0, steps, token_step, 0)
     for m in range(3):
         startf[m * width : (m + 1) * width] = start_ref[m].astype(jnp.float32)
@@ -446,16 +454,16 @@
 
     def fast_rows(c, sub):
         return pl.ds(pl.multiple_of((c * 2 + sub) * rows, 8), rows)
-
-    outw_over.wait_recv()
-    outw_share.start()
-    narrow_over.start()
 
     fast_pair = {}
     for k in every:
         fsb[k] = padded(gacc[fast_rows(chip(k), so)])
         fast_pair[k] = remote(fsb.at[k], fpr.at[k], core)
         fast_pair[k].start()
+    outw_side_in.wait_recv()
+    outw_twin.start()
+    outw_core.start()
+    narrow_side_in.start()
     fast_chip = {}
     for k in others:
         fast_pair[k].wait_recv()
@@ -519,6 +527,11 @@
         emb_ref[i] = embedded[i * half : (i + 1) * half]
         q_ref[i] = queries[i * half : (i + 1) * half]
 
+    wide_side_in.wait_recv()
+    wide_twin.start()
+    wide_core.start()
+    outw_twin.wait_recv()
+    outw_core2.start()
     fast_pair[0].wait_recv()
     gradient = gacc[fast_rows(t, s)] + fpr[0][:rows].astype(jnp.float32)
     for k in others:
@@ -534,8 +547,11 @@
     for k in others:
         gather_chip[k].start()
     gather_core[0].start()
-    wide_over.wait_recv()
-    wide_share.start()
+    narrow_side_in.wait_recv()
+    narrow_twin.start()
+    narrow_core.start()
+    wide_twin.wait_recv()
+    wide_core2.start()
     for k in others:
         gather_chip[k].wait_recv()
         gather_core[k].start()
@@ -557,23 +573,26 @@
     head_copy.start()
     own_out = head_out(q_ref[h])
     outw_load.wait()
-    outw_share.wait_recv()
+    outw_core.wait_recv()
+    outw_core2.wait_recv()
     resid = emb_ref[h].astype(jnp.float32) + dot(own_out, outw[...])
-    narrow_over.wait_recv()
-    narrow_share.start()
     head_copy.wait_recv()
     resid = resid + dot(hr[...], outw_side[...])
     normed = (resid * rms_scale(resid) * ngain_ref[...][None, :]).astype(jnp.bfloat16)
 
     wide_load.wait()
-    wide_share.wait_recv()
+    wide_core.wait_recv()
+    wide_core2.wait_recv()
     act_side[...] = gelu(dot(normed, wide_side[...])).astype(jnp.bfloat16)
     act_copy = remote(act_side, active.at[pl.ds(half, half)], side)
     act_copy.start()
     active[0:half] = gelu(dot(normed, wide[...])).astype(jnp.bfloat16)
     narrow_load.wait()
     mixed = dot(active[0:half], narrow[...], NT)
-    narrow_share.wait_recv()
+    narrow_twin.wait_recv()
+    narrow_core2.start()
+    narrow_core.wait_recv()
+    narrow_core2.wait_recv()
     after = resid + (mixed + dot(act_side[...], narrow_side[...], NT))
     truth = truth_ref[...].astype(jnp.float32)
     keep = (1 - tran_ref[...]).astype(jnp.float32).T
@@ -624,6 +643,13 @@
         dec_pair[k] = remote(dsb.at[k], dpr.at[k], core)
         dec_pair[k].start()
 
+    dec_chip = {}
+    for k in others:
+        dec_pair[k].wait_recv()
+        dps[k] = (dlf[part_rows(chip(k), s)] + dpr[k].astype(jnp.float32)).astype(jnp.bfloat16)
+        dec_chip[k] = remote(dps.at[k], drr.at[k], {"tok": chip(k)})
+        dec_chip[k].start()
+
     grad_copy.wait_recv()
     act_copy.wait_recv()
     both = jnp.concatenate([gs[...].astype(jnp.float32), gr[...].astype(jnp.float32)], axis=0)
@@ -635,12 +661,6 @@
         gsb[k] = dot(gat[chip(k) * 2 + so], active[...]).astype(jnp.bfloat16)
         nar_pair[k] = remote(gsb.at[k], gpr.at[k], core)
         nar_pair[k].start()
-    dec_chip = {}
-    for k in others:
-        dec_pair[k].wait_recv()
-        dps[k] = (dlf[part_rows(chip(k), s)] + dpr[k].astype(jnp.float32)).astype(jnp.bfloat16)
-        dec_chip[k] = remote(dps.at[k], drr.at[k], {"tok": chip(k)})
-        dec_chip[k].start()
     nar_chip = {}
     for k in others:
         mine = dot(gat[chip(k) * 2 + s], active[...])
@@ -681,14 +701,31 @@
         act_copy,
         grad_copy,
         dec_side,
-        outw_over,
-        outw_share,
-        wide_over,
-        wide_share,
-        narrow_over,
-        narrow_share,
+        outw_side_in,
+        outw_twin,
+        outw_core,
+        outw_core2,
+        wide_side_in,
+        wide_twin,
+        wide_core,
+        wide_core2,
+        narrow_side_in,
+        narrow_twin,
+        narrow_core,
+        narrow_core2,
     ):
         copy.wait_send()
+
+
+def hand_out(*refs):
+    count = len(refs) // 2
+    copies = [
+        pltpu.make_async_copy(refs[i], refs[count + i], refs[-1].at[i]) for i in range(count)
+    ]
+    for copy in copies:
+        copy.start()
+    for copy in copies:
+        copy.wait()
 
 
 def on_device_kernel(
@@ -731,7 +768,7 @@
     row_buf = pltpu.VMEM((half, model), bf16)
     dec_buf = pltpu.VMEM((tok_n, part, logit_n), bf16)
     nar_buf = pltpu.VMEM((tok_n, part, hidden), bf16)
-    copies = 4 * tok_n + 4 * (tok_n - 1) + 10
+    copies = 4 * tok_n + 4 * (tok_n - 1) + 16
     render, grad_decode, grad_narrow = pl.pallas_call(
         functools.partial(
             scene_kernel,
@@ -780,7 +817,7 @@
         + [
             pltpu.SemaphoreType.DMA((copies,)),
             pltpu.SemaphoreType.DMA((copies,)),
-            pltpu.SemaphoreType.DMA((9 + in_tokens.shape[0] // 256,)),
+            pltpu.SemaphoreType.DMA((9 + in_tokens.shape[0] // 512,)),
         ],
         compiler_params=pltpu.CompilerParams(
             collective_id=0, has_side_effects=True, vmem_limit_bytes=60 * 2**20
@@ -807,11 +844,22 @@
         narrow_weight,
         decode_weight,
     )
+    render, grad_decode, grad_narrow = pl.pallas_call(
+        hand_out,
+        out_shape=tuple(
+            jax.ShapeDtypeStruct(v.shape, v.dtype) for v in (render, grad_decode, grad_narrow)
+        ),
+        in_specs=[anywhere] * 3,
+        out_specs=(anywhere,) * 3,
+        scratch_shapes=[pltpu.SemaphoreType.DMA((3,))],
+    )(render, grad_decode, grad_narrow)
     return (render[None, None], grad_decode, grad_narrow)
 
 
 def kernel_fits(mesh):
-    return mesh.shape["head"] == 2 and mesh.shape["sub"] == 2 and mesh.shape["tok"] in (2, 4)
+    return mesh.shape["groups"] == 2 and mesh.shape["head"] == 2 and (
+        mesh.shape["sub"] == 2 and mesh.shape["tok"] in (2, 4)
+    )
 
 
 def solution(mesh):

time: 70.4 us -> 70.7 us (level); the launches traced: 70.1 us -> 69.6 us
  local copies, waits for them, and re-layouts: 4.65 us -> 0 us
  Pallas kernels: 64.1 us -> 68.3 us
    pallas_call x0 -> x1, Pallas kernels: none -> 14.5 us  [on_device_kernel(): pl.pallas_call(hand_out, out_shape=tuple((jax.ShapeDtypeStruct(v.shape, v...]
    pallas_call x1, Pallas kernels: 64.1 us -> 53.7 us  [on_device_kernel(): pl.pallas_call(functools.partial(scene_kernel, tok_n, RATE_SCALE / math.s...]
    unnamed x3 -> x0, local copies, waits for them, and re-layouts: 4.65 us -> none
where the time goes in v3:
time: 70.7 us; the launch traced here: 69.6 us
  Pallas kernels  68.3 us (97%)
  between operations  1.29 us (2%)
    pallas_call x1, Pallas kernels, on_device_kernel(): pl.pallas_call(functools.partial(scene_kernel, tok_n, RATE_SCALE / math.s...  53.7 us
    pallas_call x1, Pallas kernels, on_device_kernel(): pl.pallas_call(hand_out, out_shape=tuple((jax.ShapeDtypeStruct(v.shape, v...  14.5 us

profile of v3, /device:TPU:0, one launch (start us, length us, event | category | flops | bytes accessed | tf_op | source)
XLA Modules:
  0.0 69.6 jit_solution(14538749212576396574)
XLA Ops:
  1.3 53.7 %shard_map.211 = (bf16[96,192]{1,0:T(8,128)(2,1)}, f32[96,256]{1,0:T(8,128)}, f32[96,768]{1,0:T(8,128)}) custom-call(f32[1]{0:T(128)S(6)} %copy.23.rb_ref, s32[192]{0:T(256)} %views_ref.1, s32[192]{0:T(256)} %rays_ref.1, f32[9,32]{1,0:T(8,128)} %bitcast.18, f32[3,32]{1,0:T(4,128)} %bitcast.20, bf16[1,768]{1,0:T(2,128)(2,1)} %bitcast.19, ...), custom_call_target="tpu_custom_call" | custom-call | tf_op jit(solution)/shard_map/pallas_call | solution.py:772
  55.0 14.5 %shard_map.212 = (bf16[96,192]{1,0:T(8,128)(2,1)}, f32[96,256]{1,0:T(8,128)}, f32[96,768]{1,0:T(8,128)}) custom-call(bf16[96,192]{1,0:T(8,128)(2,1)} %get-tuple-element.9.refs_0_, f32[96,256]{1,0:T(8,128)} %get-tuple-element.10.refs_1_, f32[96,768]{1,0:T(8,128)} %get-tuple-element.11.refs_2_), custom_call_target="tpu_custom_call" | custom-call | tf_op jit(solution)/shard_map/pallas_call | solution.py:847

commit v4 on v3

--- a/solution.py
+++ b/solution.py
@@ -719,13 +719,8 @@
 
 def hand_out(*refs):
     count = len(refs) // 2
-    copies = [
-        pltpu.make_async_copy(refs[i], refs[count + i], refs[-1].at[i]) for i in range(count)
-    ]
-    for copy in copies:
-        copy.start()
-    for copy in copies:
-        copy.wait()
+    for i in range(count):
+        refs[count + i][...] = refs[i][...]
 
 
 def on_device_kernel(
@@ -849,9 +844,8 @@
         out_shape=tuple(
             jax.ShapeDtypeStruct(v.shape, v.dtype) for v in (render, grad_decode, grad_narrow)
         ),
-        in_specs=[anywhere] * 3,
-        out_specs=(anywhere,) * 3,
-        scratch_shapes=[pltpu.SemaphoreType.DMA((3,))],
+        in_specs=[vmem] * 3,
+        out_specs=(vmem,) * 3,
     )(render, grad_decode, grad_narrow)
     return (render[None, None], grad_decode, grad_narrow)
 

time: 70.7 us -> 58 us (0.82)
  the two profiles are of different devices: /device:TPU:0 before, /device:TPU:9 now
where the time goes in v4:
time: 58 us; the launch traced here: 57.8 us
  Pallas kernels  56.5 us (97%)
  between operations  1.29 us (2%)
    pallas_call x1, Pallas kernels, on_device_kernel(): pl.pallas_call(functools.partial(scene_kernel, tok_n, RATE_SCALE / math.s...  54.7 us
    pallas_call x1, Pallas kernels, on_device_kernel(): pl.pallas_call(hand_out, out_shape=tuple((jax.ShapeDtypeStruct(v.shape, v...  1.82 us

profile of v4, /device:TPU:9, one launch (start us, length us, event | category | flops | bytes accessed | tf_op | source)
XLA Modules:
  0.0 57.8 jit_solution(4698217584438673573)
XLA Ops:
  1.3 54.7 %shard_map.211 = (bf16[96,192]{1,0:T(8,128)(2,1)}, f32[96,256]{1,0:T(8,128)}, f32[96,768]{1,0:T(8,128)}) custom-call(f32[1]{0:T(128)S(6)} %copy.23.rb_ref, s32[192]{0:T(256)} %views_ref.1, s32[192]{0:T(256)} %rays_ref.1, f32[9,32]{1,0:T(8,128)} %bitcast.18, f32[3,32]{1,0:T(4,128)} %bitcast.20, bf16[1,768]{1,0:T(2,128)(2,1)} %bitcast.19, ...), custom_call_target="tpu_custom_call" | custom-call | tf_op jit(solution)/shard_map/pallas_call | solution.py:767
  56.0 1.8 %shard_map.212 = (bf16[96,192]{1,0:T(8,128)(2,1)}, f32[96,256]{1,0:T(8,128)}, f32[96,768]{1,0:T(8,128)}) custom-call(bf16[96,192]{1,0:T(8,128)(2,1)} %get-tuple-element.9.refs_0_, f32[96,256]{1,0:T(8,128)} %get-tuple-element.10.refs_1_, f32[96,768]{1,0:T(8,128)} %get-tuple-element.11.refs_2_), custom_call_target="tpu_custom_call" | custom-call | tf_op jit(solution)/shard_map/pallas_call | solution.py:842
